TPU v7x, 32 devices: a whole 2x2x4 slice. The times are simulated.
32 devices in a mesh: dp: 4 (over x, core), fsdp: 8 (over z, y).
Axes of the slice: x: 2, y: 2, z: 4, core: 2. Of those that a mesh axis runs over, the one named last changes fastest.
Arguments:
- tokens: bfloat16 [32, 512, 768], P(('dp', 'fsdp'))
- segment_ids: int32 [32, 512], P(('dp', 'fsdp')), may hold values from 0 to 5, never falling along the last dimension, each value on 1 to 256 neighbouring positions
- cotangent: bfloat16 [32, 512, 768], P(('dp', 'fsdp')), may hold values from -6 to 6
- attention_weight: float32 [4, 768, 768], P(None, 'fsdp')
- attention_first: float32 [4, 768, 768], P(None, 'fsdp'), may hold values from -0.00061035156 to 0.00061035156
- attention_second: float32 [4, 768, 768], P(None, 'fsdp'), may hold values from 9.877095e-11 to 8.466082e-10
- inner_weight: float32 [768, 3072], P('fsdp'), may hold values from -0.21875 to 0.21875
- inner_first: float32 [768, 3072], P('fsdp'), may hold values from -0.00061035156 to 0.00061035156
- inner_second: float32 [768, 3072], P('fsdp'), may hold values from 1.2699122e-11 to 5.079649e-11
- outer_weight: float32 [3072, 768], P('fsdp'), may hold values from -0.109375 to 0.109375
- outer_first: float32 [3072, 768], P('fsdp'), may hold values from -0.00061035156 to 0.00061035156
- outer_second: float32 [3072, 768], P('fsdp'), may hold values from 9.877095e-11 to 8.466082e-10
- vectors: float32 [12, 768], P(None, 'fsdp')
- vector_first: float32 [12, 768], P(None, 'fsdp'), may hold values from -0.00061035156 to 0.00061035156
- vector_second: float32 [12, 768], P(None, 'fsdp'), may hold values from 9.877095e-11 to 8.466082e-10
Outputs:
- activations: bfloat16 [32, 512, 768], P(('dp', 'fsdp'))
- input_grad: float32 [32, 512, 768], P(('dp', 'fsdp'))
- grad_norm: float32 [], replicated
- attention_new: float32 [4, 768, 768], P(None, 'fsdp')
- attention_first_new: float32 [4, 768, 768], P(None, 'fsdp')
- attention_second_new: float32 [4, 768, 768], P(None, 'fsdp')
- inner_new: float32 [768, 3072], P('fsdp')
- inner_first_new: float32 [768, 3072], P('fsdp')
- inner_second_new: float32 [768, 3072], P('fsdp')
- outer_new: float32 [3072, 768], P('fsdp')
- outer_first_new: float32 [3072, 768], P('fsdp')
- outer_second_new: float32 [3072, 768], P('fsdp')
- vectors_new: float32 [12, 768], P(None, 'fsdp')
- vector_first_new: float32 [12, 768], P(None, 'fsdp')
- vector_second_new: float32 [12, 768], P(None, 'fsdp')
- vector_grad: float32 [12, 768], P(None, 'fsdp')
Inputs may be any that keep to these rules, and one draw needn't show every extreme that they name: `segment_ids`: within a row the ids never fall; a run of one id holds at most 256 positions, and some run of each row holds exactly that many.
All inputs are finite; a program needn't handle non-finite values.
Results may differ from a plain program's by a relative error of at most 0.022.
Values may be sent and summed in bfloat16 or wider, within the bound.
A program may use at most 192 MiB of HBM per device.

v0:
```python
import functools

import jax
import jax.numpy as jnp
from jax import lax
from jax.experimental import pallas as pl
from jax.experimental.pallas import tpu as pltpu
from jax.sharding import PartitionSpec as P

HEADS = 12
STEP = 10


EPS_NORM = 1e-12
BETA_ONE = 0.9
BETA_TWO = 0.999
ADAM_EPS = 1e-08
DECAY = 0.01
RATE_MATRIX = 0.03
RATE_VECTOR = 0.5
CLIP = 1.0


def layer_norm(resid, gain, shift):
    centre = jnp.mean(resid, axis=-1, keepdims=True)
    centered = resid - centre
    spread = jnp.mean(centered * centered, axis=-1, keepdims=True)
    return centered * lax.rsqrt(spread + EPS_NORM) * gain + shift


def gelu_exact(values):
    return jax.nn.gelu(values, approximate=False)


def split_heads(matrix):
    return matrix.reshape(matrix.shape[0], HEADS, matrix.shape[1] // HEADS)


def row_scores(query_row, key_row, segment_row):
    scores = jnp.einsum(
        "qhe,khe->hqk",
        split_heads(query_row),
        split_heads(key_row),
        preferred_element_type=jnp.float32,
    )
    same_segment = segment_row[:, None] == segment_row[None, :]
    return jnp.where(same_segment[None], scores, -1000000000.0)


def attend_row(pieces):
    query_row, key_row, value_row, segment_row = pieces
    scores = row_scores(query_row, key_row, segment_row)
    row_peak = jnp.max(scores, axis=-1, keepdims=True)
    exponent = jnp.exp(scores - row_peak)
    row_total = jnp.sum(exponent, axis=-1, keepdims=True)
    softmax_rows = exponent / row_total
    mixture = jnp.einsum(
        "hqk,khe->qhe",
        softmax_rows.astype(jnp.bfloat16),
        split_heads(value_row),
        preferred_element_type=jnp.float32,
    )
    return (mixture.reshape(query_row.shape).astype(jnp.bfloat16), row_peak + jnp.log(row_total))


def attend_back(pieces):
    query_row, key_row, value_row, segment_row, log_total, context_grad = pieces
    row_shape = query_row.shape
    scores = row_scores(query_row, key_row, segment_row)
    softmax_rows = jnp.exp(scores - log_total)
    grad_heads = split_heads(context_grad)
    prob_grad = jnp.einsum(
        "qhe,khe->hqk", grad_heads, split_heads(value_row), preferred_element_type=jnp.float32
    )
    value_grad = jnp.einsum(
        "hqk,qhe->khe",
        softmax_rows.astype(jnp.bfloat16),
        grad_heads,
        preferred_element_type=jnp.float32,
    )
    row_delta = jnp.sum(prob_grad * softmax_rows, axis=-1, keepdims=True)
    score_grad = (softmax_rows * (prob_grad - row_delta)).astype(jnp.bfloat16)
    query_grad = jnp.einsum(
        "hqk,khe->qhe", score_grad, split_heads(key_row), preferred_element_type=jnp.float32
    )
    key_grad = jnp.einsum(
        "hqk,qhe->khe", score_grad, split_heads(query_row), preferred_element_type=jnp.float32
    )
    return (
        query_grad.reshape(row_shape).astype(jnp.bfloat16),
        key_grad.reshape(row_shape).astype(jnp.bfloat16),
        value_grad.reshape(row_shape).astype(jnp.bfloat16),
    )


def adam_update(weight, first, second, gradient, factor, rate):
    clipped = gradient * factor
    first_new = BETA_ONE * first + (1.0 - BETA_ONE) * clipped
    second_new = BETA_TWO * second + (1.0 - BETA_TWO) * clipped * clipped
    first_hat = first_new / (1.0 - BETA_ONE**STEP)
    second_hat = second_new / (1.0 - BETA_TWO**STEP)
    weight_new = weight - rate * (first_hat / (jnp.sqrt(second_hat) + ADAM_EPS) + DECAY * weight)
    return (weight_new, first_new, second_new)


F32, BF16 = jnp.float32, jnp.bfloat16
MESH = pl.DeviceIdType.MESH
BLOCKS = 6
CHUNKS = 6
INV_SQRT2 = 0.7071067811865476
INV_SQRT2PI = 0.3989422804014327


def dot_nn(a, b):
    return lax.dot_general(a, b, (((1,), (0,)), ((), ())), preferred_element_type=F32)


def dot_nt(a, b):
    return lax.dot_general(a, b, (((1,), (1,)), ((), ())), preferred_element_type=F32)


def dot_tn(a, b):
    return lax.dot_general(a, b, (((0,), (0,)), ((), ())), preferred_element_type=F32)


def wide(value):
    return value.astype(F32)


class Place:
    def __init__(self):
        dp, fsdp = lax.axis_index("dp"), lax.axis_index("fsdp")
        self.x, self.c, self.z, self.y = dp // 2, dp % 2, fsdp // 2, fsdp % 2

    def dev(self, x=None, c=None, z=None, y=None):
        x = self.x if x is None else x
        c = self.c if c is None else c
        z = self.z if z is None else z
        y = self.y if y is None else y
        return (x * 2 + c, z * 2 + y)

    def far(self, dz):
        return lax.rem(self.z + dz, 4)


def half(x):
    return pl.ds(pl.multiple_of(x * 384, 128), 384)


def remote(src, dst, send, recv, dev):
    return pltpu.make_async_remote_copy(
        src_ref=src, dst_ref=dst, send_sem=send, recv_sem=recv, device_id=dev, device_id_type=MESH
    )


def at_one(index):
    return index.start if isinstance(index, slice) else index


class Gather:
    def __init__(self, at, att, inn, out, sems, alpha):
        self.at, self.att, self.inn, self.out, self.alpha = at, att, inn, out, alpha
        self.zs, self.zr, self.ys, self.yr, self.xs, self.xr, self.cs, self.cr = sems

    def ref(self, i, z, y, x):
        c = self.at.c
        cols = slice(None) if x is None else half(x)
        if i < 2:
            return self.att.at[2 * i + c, z, y, :, cols]
        if i < 4:
            return self.inn.at[2 * (i - 2) + c, z, y, :, cols]
        return self.out.at[z, y, 2 * (i - 4) + c, :, cols]

    def whole(self, i, c):
        if i < 2:
            return self.att.at[2 * i + c]
        if i < 4:
            return self.inn.at[2 * (i - 2) + c]
        return self.out.at[:, :, 2 * (i - 4) + c]

    def zmove(self, i, s, right, sz):
        z = self.at.z
        dest = jnp.minimum(z + 1, 3) if right else jnp.maximum(z - 1, 0)
        r = self.ref(i, sz, self.at.y, self.at.x if self.alpha[i] == 1 else None)
        return remote(r, r, self.zs.at[i, 0 if right else 1], self.zr.at[i, at_one(sz)], self.at.dev(z=dest))

    def ymove(self, i, sz, recv=False):
        y = 1 - self.at.y if recv else self.at.y
        r = self.ref(i, sz, y, self.at.x if self.alpha[i] else None)
        return remote(r, r, self.ys.at[i], self.yr.at[i, at_one(sz)], self.at.dev(y=1 - self.at.y))

    def xmove(self, i, sz, own, recv=False):
        y = self.at.y if own else 1 - self.at.y
        x = 1 - self.at.x if recv else self.at.x
        k = 0 if own else 1
        r = self.ref(i, sz, y, x)
        return remote(r, r, self.xs.at[i, k], self.xr.at[i, k], self.at.dev(x=1 - self.at.x))

    def cmove(self, i, recv=False):
        r = self.whole(i, 1 - self.at.c if recv else self.at.c)
        return remote(r, r, self.cs.at[i], self.cr.at[i], self.at.dev(c=1 - self.at.c))

    def zown(self, i):
        z = self.at.z

        @pl.when(z < 3)
        def _():
            self.zmove(i, 0, True, z).start()

        @pl.when(z > 0)
        def _():
            self.zmove(i, 0, False, z).start()

    def yown(self, i):
        self.ymove(i, self.at.z).start()

    def arrive(self, i, s):
        z = self.at.z

        def forward(sz, right, more):
            self.zmove(i, s, right, sz).wait_recv()
            if s < 2:

                @pl.when(more)
                def _():
                    self.zmove(i, s + 1, right, sz).start()

            self.ymove(i, sz).start()
            if self.alpha[i] == 1:
                self.xmove(i, sz, True).start()

        @pl.when(z >= 1 + s)
        def _():
            forward(jnp.maximum(z - 1 - s, 0), True, z < 3)

        @pl.when(z + 1 + s <= 3)
        def _():
            forward(jnp.minimum(z + 1 + s, 3), False, z > 0)

    def across(self, i, s):
        z = self.at.z

        def one(sz):
            self.ymove(i, sz, True).wait_recv()
            if self.alpha[i]:
                self.xmove(i, sz, False).start()

        if s == 0:
            one(z)
            return

        @pl.when(z >= s)
        def _():
            one(jnp.maximum(z - s, 0))

        @pl.when(z + s <= 3)
        def _():
            one(jnp.minimum(z + s, 3))

    def join(self, i):
        if self.alpha[i]:
            self.xmove(i, slice(0, 4), False, True).wait_recv()
        if self.alpha[i] == 1:
            self.xmove(i, slice(0, 3), True, True).wait_recv()
        self.cmove(i).start()

    def have(self, i):
        self.cmove(i, True).wait_recv()

    def finish(self):
        z = self.at.z
        for i in range(BLOCKS):
            for count in (1, 2, 3):

                @pl.when(z + 1 == count)
                def _():
                    self.zmove(i, 0, True, slice(0, count)).wait_send()

                @pl.when(4 - z == count)
                def _():
                    self.zmove(i, 0, False, slice(0, count)).wait_send()

            self.ymove(i, slice(0, 4)).wait_send()
            if self.alpha[i]:
                self.xmove(i, slice(0, 4), False).wait_send()
            if self.alpha[i] == 1:
                self.xmove(i, slice(0, 3), True).wait_send()
            self.cmove(i).wait_send()


class Scatter:
    def __init__(self, at, grad, total, bufs, sems, alpha):
        self.at, self.grad, self.total, self.alpha = at, grad, total, alpha
        self.ra1, self.ra2, self.ra3, self.rb1, self.rb2, self.rb3 = bufs
        self.ss, self.rs = sems
        self.slot = [sum(1 for q in alpha[:j] if q == alpha[j]) for j in range(CHUNKS)]

    def cp(self, j, kind, k, src, dst, dev):
        return remote(src, dst, self.ss.at[j, kind], self.rs.at[j, k], dev)

    def block(self, j, c):
        return 4 * (j // 2) + 2 * c + j % 2

    def firsts(self, j, dz, own):
        n, at = self.slot[j], self.at
        z = at.far(dz)
        if self.alpha[j]:
            y = at.y if own else 1 - at.y
            return self.cp(
                j, own, dz + 4 * own, self.grad(j, z, y).at[:, half(1 - at.x)], self.ra1.at[n, z, y], at.dev(x=1 - at.x)
            )
        return self.cp(j, 0, dz, self.grad(j, z, 1 - at.y), self.rb1.at[n, z], at.dev(y=1 - at.y))

    def second(self, j, dz):
        n, at = self.slot[j], self.at
        z = at.far(dz)
        return self.cp(
            j, 2, 8 + dz, self.grad(j, z, 1 - at.y).at[:, half(at.x)], self.ra2.at[n, z], at.dev(y=1 - at.y)
        )

    def third(self, j, dz):
        n, at = self.slot[j], self.at
        z = at.far(dz)
        src = self.grad(j, z, at.y)
        if self.alpha[j]:
            return self.cp(j, 3, 12, src.at[:, half(at.x)], self.ra3.at[n, dz - 1], at.dev(z=z))
        return self.cp(j, 3, 12, src, self.rb2.at[n, dz - 1], at.dev(z=z))

    def fourth(self, j, recv=False):
        n, at = self.slot[j], self.at
        if self.alpha[j]:
            r = self.total.at[self.block(j, at.c), :, half(1 - at.x if recv else at.x)]
            return self.cp(j, 4, 13, r, r, at.dev(x=1 - at.x))
        return self.cp(j, 4, 13, self.grad(j, at.z, at.y), self.rb3.at[n], at.dev(x=1 - at.x))

    def fifth(self, j, recv=False):
        r = self.total.at[self.block(j, 1 - self.at.c if recv else self.at.c)]
        return self.cp(j, 5, 14, r, r, self.at.dev(c=1 - self.at.c))

    def s1(self, j):
        if j == 0:
            return
        for dz in (2, 1, 3, 0):
            self.firsts(j, dz, 0).start()

    def r1(self, j):
        if self.alpha[j]:
            for dz in (2, 1, 3, 0):
                self.firsts(j, dz, 1).start()

    def p(self, j, dz):
        if not self.alpha[j]:
            return
        n, at = self.slot[j], self.at
        z, y, h = at.far(dz), 1 - at.y, half(at.x)
        self.firsts(j, dz, 0).wait_recv()
        r = self.grad(j, z, y)
        r[:, h] = (wide(r[:, h]) + wide(self.ra1[n, z, y])).astype(BF16)
        self.second(j, dz).start()

    def q(self, j, dz):
        n, at = self.slot[j], self.at
        z, y, h = at.far(dz), at.y, half(at.x)
        r = self.grad(j, z, y)
        if self.alpha[j]:
            self.firsts(j, dz, 1).wait_recv()
            self.second(j, dz).wait_recv()
            r[:, h] = (wide(r[:, h]) + wide(self.ra1[n, z, y]) + wide(self.ra2[n, z])).astype(BF16)
        else:
            self.firsts(j, dz, 0).wait_recv()
            r[...] = (wide(r[...]) + wide(self.rb1[n, z])).astype(BF16)
        if dz:
            self.third(j, dz).start()

    def s4(self, j):
        n, at = self.slot[j], self.at
        landed = (self.ra3 if self.alpha[j] else self.rb2).at[n]
        remote(landed, landed, self.ss.at[j, 3], self.rs.at[j, 12], at.dev(z=at.far(1))).wait_recv()
        r = self.grad(j, at.z, at.y)
        if self.alpha[j]:
            h = half(at.x)
            total = wide(r[:, h])
            for dz in range(3):
                total = total + wide(self.ra3[n, dz])
            self.total[self.block(j, at.c), :, h] = total.astype(BF16)
        else:
            total = wide(r[...])
            for dz in range(3):
                total = total + wide(self.rb2[n, dz])
            r[...] = total.astype(BF16)
        self.fourth(j).start()

    def s5(self, j):
        n, at = self.slot[j], self.at
        self.fourth(j, True).wait_recv()
        if not self.alpha[j]:
            r = self.grad(j, at.z, at.y)
            self.total[self.block(j, at.c)] = (wide(r[...]) + wide(self.rb3[n])).astype(BF16)
        self.fifth(j).start()

    def s6(self, j):
        self.fifth(j, True).wait_recv()

    def finish(self):
        at = self.at
        for j in range(CHUNKS):
            n = self.slot[j]
            first = (self.ra2 if self.alpha[j] else self.rb1).at[n]
            last = (self.ra3 if self.alpha[j] else self.rb2).at[n]
            sent = [(0, first)]
            if self.alpha[j]:
                sent += [(1, first), (2, first)]
            for kind, like in sent + [(3, last)]:
                remote(like, like, self.ss.at[j, kind], self.rs.at[j, 0], at.dev(x=1 - at.x)).wait_send()
            self.fourth(j).wait_send()
            self.fifth(j).wait_send()


def layer_kernel(
    order, alpha_gather, alpha_scatter,
    tok_h, cot_h, seg_h, watt_h, winn_h, wout_h, vec_h,
    act_h, grad_h, total_h, vec_grad, norm,
    att, inn, out, norm_one, resid, work, pair_in, stack, hidden, outer_grad, shown, turn, turn_two,
    active, slope, probs, mask, vec, dev_one, dev_two,
    sib_in, sib_hidden, sib_active, sib_outer, sib_slope, sib_stack,
    grad_out, ra1, ra2, ra3, rb1, rb2, rb3,
    vec_parts, vec_sib, vec_x, vec_y, vec_z, norm_parts, mate_parts, total, seg_row, vec_in,
    zs, zr, ys, yr, xs, xr, cs, cr, ss, rs, bs, br, vs, vr, ws, wr, ns, nr, ls,
):
    at = Place()
    me = at.z * 2 + at.y
    ag = Gather(at, att, inn, out, (zs, zr, ys, yr, xs, xr, cs, cr), alpha_gather)

    def grad_ref(j, z, y):
        return grad_out.at[j, z, y] if j < 2 else out.at[z, y, j - 2]

    rd = Scatter(at, grad_ref, total, (ra1, ra2, ra3, rb1, rb2, rb3), (ss, rs), alpha_scatter)

    def square(ref, n=768):
        return ref[...].reshape(n, n)

    other = at.dev(c=1 - at.c)

    def to_sibling(k, src, dst):
        return remote(src, dst, bs.at[k], br.at[k], other)

    sib_tokens = to_sibling(0, pair_in.at[0], sib_in.at[0])
    sib_context = to_sibling(1, pair_in.at[1], sib_in.at[1])
    sib_hid = to_sibling(2, hidden, sib_hidden)
    sib_act = to_sibling(3, active.at[:, :, pl.ds(2 * (1 - at.c), 2)], sib_active)
    sib_og = [
        to_sibling(k, outer_grad.at[pl.ds(128 * r, 128)], sib_outer.at[pl.ds(128 * r, 128)])
        for r, k in enumerate((4, 8, 9, 10))
    ]
    sib_sl = to_sibling(5, slope.at[:, pl.ds(pl.multiple_of((1 - at.c) * 1536, 128), 1536)], sib_slope)
    sib_first = to_sibling(6, stack.at[1 - at.c], sib_stack.at[0])
    sib_last = to_sibling(7, stack.at[3 - at.c], sib_stack.at[1])

    peers = [(dz, dy) for dz in range(4) for dy in range(2) if (dz, dy) != (0, 0)]

    def peer(dz, dy):
        return at.dev(z=at.far(dz), y=lax.rem(at.y + dy, 2))

    def vec_move(k):
        dz, dy = peers[k]
        return remote(vec_parts.at[me], vec_parts.at[me], vs.at[0], vr.at[0], peer(dz, dy))

    def norm_move(k):
        return remote(norm_parts.at[me], norm_parts.at[me], ns.at[0], nr.at[0], peer(*peers[k]))

    mates = [at.dev(x=1 - at.x), at.dev(x=1 - at.x, c=1 - at.c), other]
    rank = at.x * 2 + at.c

    def mate_move(k):
        return remote(mate_parts.at[rank], mate_parts.at[rank], ns.at[1], nr.at[1], mates[k])

    def all_of(ref, count, send, recv):
        view = ref.at[pl.ds(0, count)]
        return remote(view, view, send, recv, other)

    loads = []
    for i in range(2):
        k, rows = 2 * i + at.c, pl.ds(96 * i, 96)
        cols, shard_rows = pl.ds(pl.multiple_of(768 * k, 128), 768), pl.ds(pl.multiple_of(96 * k, 96), 96)
        loads.append(pltpu.make_async_copy(watt_h.at[k], norm_one.at[rows], ls.at[3 * i]))
        loads.append(pltpu.make_async_copy(winn_h.at[:, cols], work.at[rows], ls.at[3 * i + 1]))
        loads.append(pltpu.make_async_copy(wout_h.at[shard_rows], resid.at[rows], ls.at[3 * i + 2]))
    load_tokens = pltpu.make_async_copy(tok_h, pair_in.at[0], ls.at[9])
    load_ids = pltpu.make_async_copy(seg_h, seg_row, ls.at[7])
    load_vectors = pltpu.make_async_copy(vec_h, vec_in, ls.at[8])
    load_cotangent = pltpu.make_async_copy(cot_h, stack.at[3], ls.at[10])
    store_shown = pltpu.make_async_copy(shown, act_h, ls.at[11])
    store_grad = pltpu.make_async_copy(work, grad_h, ls.at[12])

    def init():
        barrier = pltpu.get_barrier_semaphore()
        greet = [peer(dz, dy) for dz, dy in peers] + mates
        for d in greet:
            pl.semaphore_signal(barrier, inc=1, device_id=d, device_id_type=MESH)
        for k in (0, 3, 1, 4, 2, 5):
            loads[k].start()
        load_vectors.start()
        load_ids.start()
        load_tokens.start()
        load_cotangent.start()
        for i in range(2):
            loads[3 * i].wait()
            att[2 * i + at.c, at.z, at.y] = norm_one[pl.ds(96 * i, 96), :].astype(BF16)
        pl.semaphore_wait(barrier, len(greet))

    def cast_rest():
        for i in range(2):
            k, rows = 2 * i + at.c, pl.ds(96 * i, 96)
            loads[3 * i + 1].wait()
            inn[k, at.z, at.y] = work[rows, :].astype(BF16)
            loads[3 * i + 2].wait()
            out[at.z, at.y, k] = resid[rows, :].astype(BF16)
        vec_grad[...] = jnp.zeros_like(vec_grad)

    def early():
        load_vectors.wait()
        load_ids.wait()
        vec_parts[me] = jnp.zeros((16, 128), F32)
        vec_parts[me, :12, :96] = vec_in[...]
        for k in range(7):
            vec_move(k).start()
        load_tokens.wait()
        sib_tokens.start()
        ids = jnp.broadcast_to(seg_row[...].astype(F32), (512, 512))
        mask[...] = jnp.where(ids.T == ids, 1.0, 0.0)

    def vectors_here():
        all_of(vec_parts, 7, vs.at[0], vr.at[0]).wait_recv()
        full = jnp.zeros((16, 768), F32)
        row = lax.broadcasted_iota(jnp.int32, (128, 768), 0)
        col = lax.broadcasted_iota(jnp.int32, (128, 768), 1)
        for s in range(8):
            pick = jnp.where((col == row + 96 * s) & (row < 96), 1.0, 0.0).astype(BF16)
            full = full + dot_nn(vec_parts[s].astype(BF16), pick)
        vec[...] = full

    def vrow(r):
        return vec[pl.ds(r, 1), :]

    def queries_keys():
        tokens = pair_in[0]
        stack[0] = ((dot_nn(tokens, square(att.at[0])) + vrow(0)) * 0.125).astype(BF16)
        stack[2] = dot_nn(tokens, square(att.at[1])).astype(BF16)

    def values():
        stack[1] = (dot_nn(pair_in[0], square(att.at[2])) + vrow(1)).astype(BF16)

    low = lax.broadcasted_iota(jnp.int32, (512, 128), 1) < 64

    def attend(p):
        ls_ = pl.ds(128 * p, 128)
        queries, keys = stack[0, :, ls_], stack[2, :, ls_]
        values_t = stack[1, :, ls_].T
        for h in range(2):
            mine = jnp.where(low if h == 0 else ~low, keys, jnp.zeros_like(keys))
            scores = jnp.where(mask[...] > 0.5, dot_nt(mine, queries), -1000000000.0)
            peak = jnp.max(scores, axis=0, keepdims=True)
            exponent = jnp.exp(scores - peak)
            scale = 1.0 / jnp.sum(exponent, axis=0, keepdims=True)
            weights = (exponent * scale).astype(BF16)
            probs[2 * p + h] = weights
            turn[pl.ds(128 * p + 64 * h, 64), :] = dot_nn(values_t[64 * h : 64 * h + 64], weights).astype(BF16)

    def norm_stats(value):
        centre = jnp.mean(value, axis=1, keepdims=True)
        centered = value - centre
        spread = jnp.mean(centered * centered, axis=1, keepdims=True)
        scale = lax.rsqrt(spread + EPS_NORM)
        return centered * scale, scale

    def project_out():
        pair_in[1] = turn[...].T
        sib_context.start()
        resid[...] = wide(pair_in[0]) + dot_nn(pair_in[1], square(att.at[3])) + vrow(2)
        for r in range(4):
            rows = pl.ds(128 * r, 128)
            normed, scale = norm_stats(resid[rows, :])
            norm_one[rows, :] = normed
            dev_one[rows, :] = scale
            hidden[rows, :] = (normed * vrow(3) + vrow(4)).astype(BF16)
        sib_hid.start()

    def feed_in(q):
        work[...] = dot_nn(hidden[...], square(inn.at[q])) + vrow(5 + q)
        for r in range(4):
            rows = pl.ds(128 * r, 128)
            value = work[rows, :]
            share = 0.5 * (1.0 + lax.erf(value * INV_SQRT2))
            shown[rows, :] = (value * share).astype(BF16)
            density = jnp.exp(-0.5 * value * value) * INV_SQRT2PI
            slope[rows, 768 * q : 768 * q + 768] = (share + value * density).astype(BF16)
        active[q] = shown[...].T.reshape(2, 4, 96, 512)

    def feed_out(part):
        if part == 4:
            sib_act.start()
            resid[...] = norm_one[...] * vrow(3) + vrow(4) + vrow(9)
        q = 2 * (part - 4)
        for n in range(3):
            cols = slice(256 * n, 256 * n + 256)
            resid[:, cols] += dot_tn(
                active[:, :, q : q + 2].reshape(1536, 512), out[:, :, q : q + 2, :, cols].reshape(1536, 256)
            )

    def end_norm():
        load_cotangent.wait()
        sums = [jnp.zeros((1, 768), F32) for _ in range(3)]
        for r in range(4):
            rows = pl.ds(128 * r, 128)
            normed, scale = norm_stats(resid[rows, :])
            shown[rows, :] = (normed * vrow(10) + vrow(11)).astype(BF16)
            given = wide(stack[3, rows, :])
            scaled = given * vrow(10)
            back = scale * (
                scaled
                - jnp.mean(scaled, axis=1, keepdims=True)
                - normed * jnp.mean(scaled * normed, axis=1, keepdims=True)
            )
            work[rows, :] = back
            low_back = back.astype(BF16)
            outer_grad[rows, :] = low_back
            sib_og[r].start()
            for k, term in enumerate((wide(low_back), given * normed, given)):
                sums[k] = sums[k] + jnp.sum(term, axis=0, keepdims=True)
        for k in range(3):
            vec_grad[9 + k : 10 + k, :] = sums[k]
        store_shown.start()

    def inner_back(q):
        cols = slice(768 * q, 768 * q + 768)
        resid[...] = dot_nt(outer_grad[...], out[q].reshape(768, 768))
        total_row = jnp.zeros((1, 768), F32)
        for r in range(4):
            rows = pl.ds(128 * r, 128)
            value = (resid[rows, :] * wide(slope[rows, cols])).astype(BF16)
            slope[rows, cols] = value
            total_row = total_row + jnp.sum(wide(value), axis=0, keepdims=True)
        vec_grad[5 + q : 6 + q, :] = total_row
        if q == 3:
            sib_sl.start()

    def put_chunk(j, value):
        value = value.astype(BF16).reshape(4, 2, 96, 768)
        if j < 2:
            grad_out[j] = value
        else:
            out[:, :, j - 2] = value

    def chunk_out(j):
        if j == 0:
            sib_act.wait_recv()
            for cp in sib_og:
                cp.wait_recv()
            for dz in (2, 1, 3, 0):
                z = at.far(dz)
                mine = active[z, :, pl.ds(2 * at.c, 1)].reshape(192, 512)
                theirs = sib_active[z, :, 0].reshape(192, 512)
                value = dot_nn(mine, outer_grad[...]) + dot_nn(theirs, sib_outer[...])
                grad_out[0, z] = value.astype(BF16).reshape(2, 96, 768)
                rd.firsts(0, dz, 0).start()
            return
        mine = active[:, :, pl.ds(2 * at.c + j, 1)].reshape(768, 512)
        theirs = sib_active[:, :, j].reshape(768, 512)
        put_chunk(j, dot_nn(mine, outer_grad[...]) + dot_nn(theirs, sib_outer[...]))

    def chunk_in(j):
        if j == 2:
            sib_hid.wait_recv()
            sib_sl.wait_recv()
        cols = pl.ds(pl.multiple_of(at.c * 1536 + 768 * (j - 2), 128), 768)
        put_chunk(
            j,
            dot_tn(hidden[...], slope[:, cols])
            + dot_tn(sib_hidden[...], sib_slope[:, 768 * (j - 2) : 768 * (j - 1)]),
        )

    def chunk_attention(j):
        if j == 4:
            sib_tokens.wait_recv()
            sib_first.wait_recv()
            value = dot_tn(pair_in[0], stack[at.c]) + dot_tn(sib_in[0], sib_stack[0])
            put_chunk(j, value * jnp.where(at.c == 0, 0.125, 1.0))
        else:
            sib_context.wait_recv()
            sib_last.wait_recv()
            put_chunk(j, dot_tn(pair_in[at.c], stack[2 + at.c]) + dot_tn(sib_in[at.c], sib_stack[1]))

    def hidden_back(q):
        work[...] += dot_nt(slope[:, 768 * q : 768 * q + 768], square(inn.at[q]))

    def middle_norm():
        sums = [jnp.zeros((1, 768), F32) for _ in range(3)]
        for r in range(4):
            rows = pl.ds(128 * r, 128)
            given = work[rows, :]
            normed = norm_one[rows, :]
            scaled = given * vrow(3)
            back = dev_one[rows, :] * (
                scaled
                - jnp.mean(scaled, axis=1, keepdims=True)
                - normed * jnp.mean(scaled * normed, axis=1, keepdims=True)
            )
            work[rows, :] = back
            low_back = back.astype(BF16)
            stack[3, rows, :] = low_back
            for k, term in enumerate((wide(low_back), given * normed, given)):
                sums[k] = sums[k] + jnp.sum(term, axis=0, keepdims=True)
        for k in range(3):
            vec_grad[2 + k : 3 + k, :] = sums[k]

    def context_back():
        store_shown.wait()
        shown[...] = dot_nt(stack[3], square(att.at[3])).astype(BF16)

    def attend_back(p):
        ls_ = pl.ds(128 * p, 128)
        queries, keys, vals, given = stack[0, :, ls_], stack[2, :, ls_], stack[1, :, ls_], shown[:, ls_]
        keys_t = keys.T
        value_grads, key_grads = [], []
        for h in range(2):
            mine = jnp.where(low if h == 0 else ~low, vals, jnp.zeros_like(vals))
            prob_grad = dot_nt(mine, given)
            weights = probs[2 * p + h]
            wide_weights = wide(weights)
            delta = jnp.sum(prob_grad * wide_weights, axis=0, keepdims=True)
            score_grad = (wide_weights * (prob_grad - delta)).astype(BF16)
            value_grads.append(dot_nn(weights, given))
            key_grads.append(dot_nn(score_grad, queries))
            turn[pl.ds(128 * p + 64 * h, 64), :] = dot_nn(keys_t[64 * h : 64 * h + 64], score_grad).astype(BF16)
        stack[1, :, ls_] = jnp.where(low, value_grads[0], value_grads[1]).astype(BF16)
        stack[2, :, ls_] = jnp.where(low, key_grads[0], key_grads[1]).astype(BF16)

    def queries_back():
        stack[0] = turn[...].T
        sib_first.start()
        sib_last.start()
        vec_grad[0:1, :] = 0.125 * jnp.sum(wide(stack[0]), axis=0, keepdims=True)
        vec_grad[1:2, :] = jnp.sum(wide(stack[1]), axis=0, keepdims=True)

    def input_back():
        work[...] += (
            0.125 * dot_nt(stack[0], square(att.at[0]))
            + dot_nt(stack[2], square(att.at[1]))
            + dot_nt(stack[1], square(att.at[2]))
        )
        store_grad.start()

    def vec_sum(k):
        if k == 0:
            return remote(vec_grad, vec_sib, ws.at[0], wr.at[0], other)
        if k == 1:
            return remote(vec_grad, vec_x, ws.at[1], wr.at[1], at.dev(x=1 - at.x))
        if k == 2:
            return remote(vec_grad, vec_y, ws.at[2], wr.at[2], at.dev(y=1 - at.y))
        return remote(vec_z.at[at.z], vec_z.at[at.z], ws.at[3], wr.at[3], at.dev(z=at.far(k - 2)))

    def vec_step(k):
        if k == 0:
            vec_sum(0).start()
        elif k <= 2:
            vec_sum(k - 1).wait()
            vec_grad[...] += (vec_sib if k == 1 else vec_x)[...]
            vec_sum(k).start()
        elif k == 3:
            vec_sum(2).wait()
            vec_z[at.z] = vec_grad[...] + vec_y[...]
            for m in (3, 4, 5):
                vec_sum(m).start()
        else:
            all_of(vec_z, 3, ws.at[3], wr.at[3]).wait()
            vec_grad[...] = (vec_z[0] + vec_z[1]) + (vec_z[2] + vec_z[3])

    def norm_step(k):
        if k == 0:
            part = jnp.zeros((96, 384), F32)
            for j in range(CHUNKS):
                value = wide(total[rd.block(j, at.c), :, half(at.x)])
                part = part + value * value
            mate_parts[rank] = jnp.full((8, 128), jnp.sum(part), F32)
            for m in range(3):
                mate_move(m).start()
        elif k == 1:
            all_of(mate_parts, 3, ns.at[1], nr.at[1]).wait_recv()
            norm_parts[me] = (mate_parts[0] + mate_parts[1]) + (mate_parts[2] + mate_parts[3])
            for m in range(7):
                norm_move(m).start()
        else:
            own = jnp.sum(vec_grad[...] * vec_grad[...])
            all_of(norm_parts, 7, ns.at[0], nr.at[0]).wait_recv()
            sums = norm_parts[0]
            for s in range(1, 8):
                sums = sums + norm_parts[s]
            norm[...] = sums + own

    def chunk_done(j):
        rd.s6(j)
        for c in range(2):
            b = rd.block(j, c)
            pltpu.make_async_copy(total.at[b], total_h.at[b], ls.at[6]).start()

    def finish():
        all_of(vec_parts, 7, vs.at[0], vr.at[0]).wait_send()
        all_of(norm_parts, 7, ns.at[0], nr.at[0]).wait_send()
        all_of(mate_parts, 3, ns.at[1], nr.at[1]).wait_send()
        for cp in (sib_tokens, sib_context, sib_hid, sib_act, *sib_og, sib_sl, sib_first, sib_last):
            cp.wait_send()
        pltpu.make_async_copy(total, total_h, ls.at[6]).wait()
        store_grad.wait()
        rd.finish()

    run = {
        "init": init, "early": early, "vec": vectors_here, "qk": queries_keys, "v": values, "wo": project_out,
        "ln2": end_norm, "ln1": middle_norm, "dc": context_back, "dq": queries_back,
        "ig": input_back, "init2": cast_rest, "fin": finish, "agf": ag.finish,
    }
    steps = {
        "at": attend, "ab": attend_back, "F": feed_in, "o": feed_out, "D": inner_back, "H": hidden_back, "V": vec_step,
        "G": lambda j: (chunk_out, chunk_in, chunk_attention)[j // 2](j),
        "s1": rd.s1, "r1": rd.r1, "s4": rd.s4, "s5": rd.s5, "s6": chunk_done, "N": norm_step,
        "zown": ag.zown, "yown": ag.yown, "f": ag.join, "g": ag.have,
    }
    for k in range(4):
        steps[f"p{k}"] = functools.partial(rd.p, dz=k)
        steps[f"q{k}"] = functools.partial(rd.q, dz=k)
        steps[f"a{k}"] = functools.partial(ag.arrive, s=k)
        steps[f"t{k}"] = functools.partial(ag.across, s=k)
    for name, index in order:
        if name in run:
            run[name]()
        else:
            steps[name](index)


def whole_layer(tokens, cotangent, segments, watt, winn, wout, vectors_low, order, alpha_gather, alpha_scatter):
    na = max(1, sum(alpha_scatter))
    nb = max(1, CHUNKS - sum(alpha_scatter))
    vmem, dma = pltpu.VMEM, pltpu.SemaphoreType.DMA
    flat = (512, 768)
    scratch = [
        vmem((4, 4, 2, 96, 768), BF16), vmem((4, 4, 2, 96, 768), BF16), vmem((4, 2, 4, 96, 768), BF16),
        vmem(flat, F32), vmem(flat, F32), vmem(flat, F32),
        vmem((2,) + flat, BF16), vmem((4,) + flat, BF16), vmem(flat, BF16), vmem(flat, BF16), vmem(flat, BF16),
        vmem((768, 512), BF16), vmem((8, 128), BF16),
        vmem((4, 2, 4, 96, 512), BF16), vmem((512, 3072), BF16), vmem((12, 512, 512), BF16),
        vmem((512, 512), F32), vmem((16, 768), F32), vmem((512, 1), F32), vmem((8, 128), F32),
        vmem((2,) + flat, BF16), vmem(flat, BF16), vmem((4, 2, 2, 96, 512), BF16), vmem(flat, BF16),
        vmem((512, 1536), BF16), vmem((2,) + flat, BF16),
        vmem((2, 4, 2, 96, 768), BF16),
        vmem((na, 4, 2, 96, 384), BF16), vmem((na, 4, 96, 384), BF16), vmem((na, 3, 96, 384), BF16),
        vmem((nb, 4, 96, 768), BF16), vmem((nb, 3, 96, 768), BF16), vmem((nb, 96, 768), BF16),
        vmem((8, 16, 128), F32), vmem((16, 768), F32), vmem((16, 768), F32), vmem((16, 768), F32),
        vmem((4, 16, 768), F32), vmem((8, 8, 128), F32), vmem((4, 8, 128), F32), vmem((12, 96, 768), BF16),
        vmem((1, 512), jnp.int32), vmem((12, 96), F32),
    ]
    for n in (
        (BLOCKS, 2), (BLOCKS, 4), (BLOCKS,), (BLOCKS, 4), (BLOCKS, 2), (BLOCKS, 2), (BLOCKS,), (BLOCKS,),
        (CHUNKS, 6), (CHUNKS, 15), (11,), (11,), (1,), (1,), (4,), (4,), (2,), (2,), (13,),
    ):
        scratch.append(dma(n))
    local, far = pl.BlockSpec(memory_space=pltpu.VMEM), pl.BlockSpec(memory_space=pl.ANY)
    return pl.pallas_call(
        functools.partial(layer_kernel, order, alpha_gather, alpha_scatter),
        out_shape=[
            jax.ShapeDtypeStruct(flat, BF16), jax.ShapeDtypeStruct(flat, F32),
            jax.ShapeDtypeStruct((12, 96, 768), BF16), jax.ShapeDtypeStruct((16, 768), F32),
            jax.ShapeDtypeStruct((8, 128), F32),
        ],
        in_specs=[far] * 7,
        out_specs=[far, far, far, local, local],
        scratch_shapes=scratch,
        compiler_params=pltpu.CompilerParams(
            collective_id=0, has_side_effects=True, vmem_limit_bytes=63 * 2**20
        ),
        name="layer",
    )(
        tokens, cotangent, segments.reshape(1, 512), watt, winn, wout, vectors_low
    )


def adam_kernel(
    act_h, back_h, total_h, norm_ref, vec_ref,
    att_w, att_m, att_v, inn_w, inn_m, inn_v, out_w, out_m, out_v, vec_w, vec_m, vec_v,
    act_new, back_new, norm_new, att_wn, att_mn, att_vn, inn_wn, inn_mn, inn_vn, out_wn, out_mn, out_vn,
    vec_wn, vec_mn, vec_vn, vec_gn,
    hold, grads, act, back, loads, stores,
):
    parts = []
    for p in range(6):
        k = 2 * (p % 2)
        rows, cols = pl.ds(96 * k, 192), pl.ds(768 * k, 1536)
        if p < 2:
            parts.append((8 + k, [[r.at[pl.ds(k, 2)] for r in (w, n)] for w, n in (
                (att_w, att_wn), (att_m, att_mn), (att_v, att_vn))]))
        elif p < 4:
            parts.append((k, [[r.at[rows] for r in (w, n)] for w, n in (
                (out_w, out_wn), (out_m, out_mn), (out_v, out_vn))]))
        else:
            parts.append((4 + k, [[r.at[:, cols] for r in (w, n)] for w, n in (
                (inn_w, inn_wn), (inn_m, inn_mn), (inn_v, inn_vn))]))

    def slot(p, m):
        if p < 2:
            return hold[0].at[p, m]
        return hold[1].at[p - 2, m] if p < 4 else hold[2].at[p - 4, m]

    def load(p, m):
        return pltpu.make_async_copy(parts[p][1][m][0], slot(p, m), loads.at[p, m])

    def store(p, m):
        return pltpu.make_async_copy(slot(p, m), parts[p][1][m][1], stores.at[p, m])

    load_grads = pltpu.make_async_copy(total_h, grads, loads.at[6, 0])
    moves = [
        (pltpu.make_async_copy(src, mid, loads.at[6, k]), pltpu.make_async_copy(mid, dst, stores.at[6, k]))
        for k, (src, mid, dst) in enumerate(((act_h, act, act_new), (back_h, back, back_new)), 1)
    ]
    load_grads.start()
    for p in range(6):
        for m in range(3):
            load(p, m).start()
        if p == 1:
            for first, _ in moves:
                first.start()
    length = jnp.sqrt(norm_ref[0:1, 0:1])
    factor = CLIP / (length + 1e-06)
    norm_new[...] = length
    shard = vec_w.shape[1]
    own = lax.axis_index("fsdp")
    grad = jnp.zeros(vec_w.shape, F32)
    for s in range(8):
        grad = grad + jnp.where(own == s, vec_ref[:12, shard * s : shard * s + shard], 0.0)
    found = adam_update(vec_w[...], vec_m[...], vec_v[...], grad, factor, RATE_VECTOR)
    for ref, value in zip((vec_wn, vec_mn, vec_vn), found):
        ref[...] = value
    vec_gn[...] = grad * factor
    load_grads.wait()
    for p in range(6):
        for m in range(3):
            load(p, m).wait()
        for k in range(2):
            grad = grads[parts[p][0] + k].astype(F32)
            if p < 2:
                views = [slot(p, m).at[k] for m in range(3)]
            elif p < 4:
                views = [slot(p, m).at[pl.ds(96 * k, 96)] for m in range(3)]
            else:
                views = [slot(p, m).at[:, pl.ds(768 * k, 768)] for m in range(3)]
            found = adam_update(*(v[...] for v in views), grad, factor, RATE_MATRIX)
            for view, value in zip(views, found):
                view[...] = value
        for m in range(3):
            store(p, m).start()
        if p == 2:
            for first, second in moves:
                first.wait()
                second.start()
    for p in range(6):
        for m in range(3):
            store(p, m).wait()
    for _, second in moves:
        second.wait()


def adam_step(activations, input_grad, norm, vec_grad, total, att, inn, out, vec):
    near, far = pl.BlockSpec(memory_space=pltpu.VMEM), pl.BlockSpec(memory_space=pl.ANY)
    like = [jax.ShapeDtypeStruct(a.shape, F32) for a in (*att, *inn, *out, *vec, vec[0])]
    vmem, dma = pltpu.VMEM, pltpu.SemaphoreType.DMA
    hold = (vmem((2, 3, 2, 96, 768), F32), vmem((2, 3, 192, 768), F32), vmem((2, 3, 96, 1536), F32))
    return pl.pallas_call(
        adam_kernel,
        out_shape=[
            jax.ShapeDtypeStruct(activations.shape, BF16), jax.ShapeDtypeStruct(input_grad.shape, F32),
            jax.ShapeDtypeStruct((1, 1), F32), *like,
        ],
        in_specs=[far, far, far, near, near, *[far] * 9, *[near] * 3],
        out_specs=[far, far, near, *[far] * 9, *[near] * 4],
        scratch_shapes=[
            hold, vmem(total.shape, BF16), vmem(activations.shape, BF16), vmem(input_grad.shape, F32),
            dma((7, 3)), dma((7, 3)),
        ],
        compiler_params=pltpu.CompilerParams(vmem_limit_bytes=63 * 2**20),
        name="adam",
    )(activations, input_grad, total, norm, vec_grad, *att, *inn, *out, *vec)


ALPHA_GATHER = (1, 1, 0, 1, 1, 0)
ALPHA_SCATTER = (0, 1, 0, 1, 1, 1)
ORDER = (
    ("init", 0), ("yown", 0), ("zown", 0), ("yown", 1), ("init2", 0), ("yown", 2), ("zown", 1), ("early", 0),
    ("t0", 0), ("a0", 0), ("a0", 1), ("zown", 2), ("t0", 1), ("a1", 0), ("zown", 3), ("yown", 3), ("t1", 0),
    ("a1", 1), ("a0", 2), ("t1", 1), ("t2", 0), ("zown", 4), ("t2", 1), ("a2", 0), ("a2", 1), ("yown", 4),
    ("a0", 3), ("t3", 0), ("yown", 5), ("t3", 1), ("t0", 3), ("zown", 5), ("a1", 3), ("a1", 2), ("f", 0),
    ("f", 1), ("g", 0), ("a0", 4), ("a2", 3), ("vec", 0), ("qk", 0), ("t1", 3), ("g", 1), ("t0", 2), ("v", 0),
    ("a1", 4), ("at", 0), ("t1", 2), ("at", 1), ("t2", 3), ("a2", 2), ("a0", 5), ("t2", 2), ("at", 2),
    ("t3", 3), ("a2", 4), ("at", 3), ("t3", 2), ("t0", 4), ("f", 2), ("a1", 5), ("at", 4), ("t1", 4),
    ("f", 3), ("t0", 5), ("at", 5), ("t2", 4), ("wo", 0), ("t3", 4), ("g", 2), ("g", 3), ("a2", 5), ("F", 2),
    ("F", 3), ("f", 4), ("t1", 5), ("F", 0), ("t2", 5), ("t3", 5), ("f", 5), ("g", 4), ("F", 1), ("g", 5),
    ("o", 4), ("o", 5), ("ln2", 0), ("agf", 0), ("D", 1), ("G", 0), ("s1", 0), ("G", 1), ("p2", 0), ("s1", 1),
    ("r1", 1), ("D", 0), ("D", 2), ("D", 3), ("p3", 0), ("p1", 0), ("r1", 0), ("H", 0), ("q2", 0), ("H", 1),
    ("H", 2), ("G", 2), ("G", 3), ("s1", 2), ("r1", 2), ("p1", 2), ("H", 3), ("ln1", 0), ("p2", 2), ("q3", 0),
    ("dc", 0), ("p2", 1), ("p3", 2), ("s1", 3), ("ab", 0), ("p0", 0), ("ab", 1), ("r1", 3), ("ab", 2),
    ("ab", 3), ("q2", 2), ("ab", 4), ("ab", 5), ("dq", 0), ("q1", 0), ("p1", 3), ("p3", 1), ("q0", 0),
    ("G", 4), ("s1", 4), ("p1", 1), ("p3", 3), ("q2", 1), ("p0", 2), ("q3", 2), ("V", 0), ("q1", 2),
    ("p0", 3), ("G", 5), ("q1", 3), ("p2", 3), ("p1", 4), ("s1", 5), ("ig", 0), ("V", 1), ("p0", 1),
    ("q3", 3), ("r1", 4), ("q3", 1), ("q1", 1), ("q0", 3), ("r1", 5), ("p3", 4), ("q2", 3), ("p2", 4),
    ("q0", 1), ("p2", 5), ("p1", 5), ("V", 2), ("s4", 0), ("q1", 4), ("p0", 4), ("q2", 4), ("q0", 4),
    ("q2", 5), ("q0", 2), ("p3", 5), ("s4", 2), ("s4", 3), ("q1", 5), ("p0", 5), ("q3", 5), ("q3", 4),
    ("q0", 5), ("s4", 1), ("V", 3), ("s4", 5), ("s5", 0), ("s5", 2), ("s4", 4), ("s5", 3), ("N", 0), ("V", 4),
    ("s5", 1), ("s5", 5), ("N", 1), ("s6", 3), ("s6", 0), ("s6", 1), ("s5", 4), ("s6", 4), ("s6", 2),
    ("N", 2), ("s6", 5), ("fin", 0),
)

def plain_body(
    tokens,
    segment_ids,
    cotangent,
    attention_weight,
    attention_first,
    attention_second,
    inner_weight,
    inner_first,
    inner_second,
    outer_weight,
    outer_first,
    outer_second,
    vectors,
    vector_first,
    vector_second,
):
    row_count, seq_length, model_width = tokens.shape
    token_count = row_count * seq_length
    flat_rows = tokens.reshape(token_count, model_width)
    shards = (
        attention_weight.astype(jnp.bfloat16),
        inner_weight.astype(jnp.bfloat16),
        outer_weight.astype(jnp.bfloat16),
        vectors.astype(jnp.bfloat16),
    )
    attention_full, inner_full, outer_full, vector_full = (
        lax.all_gather(shards[0], "fsdp", axis=1, tiled=True),
        lax.all_gather(shards[1], "fsdp", axis=0, tiled=True),
        lax.all_gather(shards[2], "fsdp", axis=0, tiled=True),
        lax.all_gather(shards[3], "fsdp", axis=1, tiled=True),
    )
    vector_rows = vector_full.astype(jnp.float32)
    bias_query = vector_rows[0]
    bias_value = vector_rows[1]
    bias_output = vector_rows[2]
    gain_one = vector_rows[3]
    shift_one = vector_rows[4]
    bias_inner = vector_rows[5:9].reshape(-1)
    bias_outer = vector_rows[9]
    gain_two = vector_rows[10]
    shift_two = vector_rows[11]
    projected = jnp.einsum(
        "td,kde->kte", flat_rows, attention_full[:3], preferred_element_type=jnp.float32
    )
    queries = ((projected[0] + bias_query) * 0.125).astype(jnp.bfloat16)
    key_rows = projected[1].astype(jnp.bfloat16)
    value_rows = (projected[2] + bias_value).astype(jnp.bfloat16)
    row_view = (row_count, seq_length, model_width)
    query_view = queries.reshape(row_view)
    key_view = key_rows.reshape(row_view)
    value_view = value_rows.reshape(row_view)
    context, log_totals = lax.map(attend_row, (query_view, key_view, value_view, segment_ids))
    context_flat = context.reshape(token_count, model_width)
    attention_out = (
        jnp.dot(context_flat, attention_full[3], preferred_element_type=jnp.float32) + bias_output
    )
    sum_one = flat_rows.astype(jnp.float32) + attention_out
    hidden_one, norm_one_back = jax.vjp(layer_norm, sum_one, gain_one, shift_one)
    hidden_low = hidden_one.astype(jnp.bfloat16)
    inner_pre = jnp.dot(hidden_low, inner_full, preferred_element_type=jnp.float32) + bias_inner
    activated, gelu_back = jax.vjp(gelu_exact, inner_pre)
    activated_low = activated.astype(jnp.bfloat16)
    outer_pre = jnp.dot(activated_low, outer_full, preferred_element_type=jnp.float32) + bias_outer
    sum_two = hidden_one + outer_pre
    output, norm_two_back = jax.vjp(layer_norm, sum_two, gain_two, shift_two)
    activations = output.astype(jnp.bfloat16).reshape(row_view)
    attention_back, inner_back, outer_back = (
        lax.all_gather(shards[0], "fsdp", axis=1, tiled=True),
        lax.all_gather(shards[1], "fsdp", axis=0, tiled=True),
        lax.all_gather(shards[2], "fsdp", axis=0, tiled=True),
    )
    output_grad = cotangent.reshape(token_count, model_width).astype(jnp.float32)
    sum_two_grad, gain_two_grad, shift_two_grad = norm_two_back(output_grad)
    outer_grad = sum_two_grad.astype(jnp.bfloat16)
    outer_weight_grad = jnp.einsum(
        "tf,td->fd", activated_low, outer_grad, preferred_element_type=jnp.float32
    )
    bias_outer_grad = jnp.sum(outer_grad.astype(jnp.float32), axis=0)
    activated_grad = jnp.einsum(
        "td,fd->tf", outer_grad, outer_back, preferred_element_type=jnp.float32
    )
    (inner_raw_grad,) = gelu_back(activated_grad)
    inner_grad = inner_raw_grad.astype(jnp.bfloat16)
    inner_weight_grad = jnp.einsum(
        "td,tf->df", hidden_low, inner_grad, preferred_element_type=jnp.float32
    )
    bias_inner_grad = jnp.sum(inner_grad.astype(jnp.float32), axis=0)
    hidden_one_grad = sum_two_grad + jnp.einsum(
        "tf,df->td", inner_grad, inner_back, preferred_element_type=jnp.float32
    )
    sum_one_grad, gain_one_grad, shift_one_grad = norm_one_back(hidden_one_grad)
    attention_grad = sum_one_grad.astype(jnp.bfloat16)
    output_weight_grad = jnp.einsum(
        "td,te->de", context_flat, attention_grad, preferred_element_type=jnp.float32
    )
    bias_output_grad = jnp.sum(attention_grad.astype(jnp.float32), axis=0)
    context_grad = jnp.einsum(
        "te,de->td", attention_grad, attention_back[3], preferred_element_type=jnp.float32
    ).astype(jnp.bfloat16)
    query_grad, key_grad, value_grad = lax.map(
        attend_back,
        (query_view, key_view, value_view, segment_ids, log_totals, context_grad.reshape(row_view)),
    )
    query_grad = query_grad.reshape(token_count, model_width)
    key_grad = key_grad.reshape(token_count, model_width)
    value_grad = value_grad.reshape(token_count, model_width)
    grad_stack = jnp.stack([query_grad, key_grad, value_grad])
    projection_grad = jnp.einsum(
        "td,kte->kde", flat_rows, grad_stack, preferred_element_type=jnp.float32
    )
    projection_grad = projection_grad * jnp.array([0.125, 1.0, 1.0], jnp.float32)[:, None, None]
    attention_weight_grad = jnp.concatenate([projection_grad, output_weight_grad[None]], axis=0)
    bias_query_grad = 0.125 * jnp.sum(query_grad.astype(jnp.float32), axis=0)
    bias_value_grad = jnp.sum(value_grad.astype(jnp.float32), axis=0)
    token_grad = sum_one_grad + 0.125 * jnp.einsum(
        "te,de->td", query_grad, attention_back[0], preferred_element_type=jnp.float32
    )
    token_grad = token_grad + jnp.einsum(
        "kte,kde->td", grad_stack[1:], attention_back[1:3], preferred_element_type=jnp.float32
    )
    input_grad = token_grad.reshape(row_view)
    vector_grad = jnp.concatenate(
        [
            jnp.stack(
                [bias_query_grad, bias_value_grad, bias_output_grad, gain_one_grad, shift_one_grad]
            ),
            bias_inner_grad.reshape(4, model_width),
            jnp.stack([bias_outer_grad, gain_two_grad, shift_two_grad]),
        ],
        axis=0,
    )
    shard_grads = (
        lax.psum_scatter(
            attention_weight_grad.astype(jnp.bfloat16), "fsdp", scatter_dimension=1, tiled=True
        ).astype(jnp.float32),
        lax.psum_scatter(
            inner_weight_grad.astype(jnp.bfloat16), "fsdp", scatter_dimension=0, tiled=True
        ).astype(jnp.float32),
        lax.psum_scatter(
            outer_weight_grad.astype(jnp.bfloat16), "fsdp", scatter_dimension=0, tiled=True
        ).astype(jnp.float32),
        lax.psum_scatter(
            vector_grad.astype(jnp.bfloat16), "fsdp", scatter_dimension=1, tiled=True
        ).astype(jnp.float32),
    )
    summed = (
        lax.psum(shard_grads[0].astype(jnp.bfloat16), "dp").astype(jnp.float32),
        lax.psum(shard_grads[1].astype(jnp.bfloat16), "dp").astype(jnp.float32),
        lax.psum(shard_grads[2].astype(jnp.bfloat16), "dp").astype(jnp.float32),
        lax.psum(shard_grads[3].astype(jnp.bfloat16), "dp").astype(jnp.float32),
    )
    local_squares = (
        jnp.sum(summed[0] * summed[0])
        + jnp.sum(summed[1] * summed[1])
        + jnp.sum(summed[2] * summed[2])
        + jnp.sum(summed[3] * summed[3])
    )
    total_squares = lax.psum(local_squares, "fsdp")
    grad_norm = jnp.sqrt(total_squares)
    factor = CLIP / (grad_norm + 1e-06)
    attention_new, attention_first_new, attention_second_new = adam_update(
        attention_weight, attention_first, attention_second, summed[0], factor, RATE_MATRIX
    )
    inner_new, inner_first_new, inner_second_new = adam_update(
        inner_weight, inner_first, inner_second, summed[1], factor, RATE_MATRIX
    )
    outer_new, outer_first_new, outer_second_new = adam_update(
        outer_weight, outer_first, outer_second, summed[2], factor, RATE_MATRIX
    )
    vectors_new, vector_first_new, vector_second_new = adam_update(
        vectors, vector_first, vector_second, summed[3], factor, RATE_VECTOR
    )
    clipped_vectors = summed[3] * factor
    return (
        activations,
        input_grad,
        grad_norm,
        attention_new,
        attention_first_new,
        attention_second_new,
        inner_new,
        inner_first_new,
        inner_second_new,
        outer_new,
        outer_first_new,
        outer_second_new,
        vectors_new,
        vector_first_new,
        vector_second_new,
        clipped_vectors,
    )


def fused_body(
    tokens,
    segment_ids,
    cotangent,
    attention_weight,
    attention_first,
    attention_second,
    inner_weight,
    inner_first,
    inner_second,
    outer_weight,
    outer_first,
    outer_second,
    vectors,
    vector_first,
    vector_second,
):
    _, seq_length, model_width = tokens.shape
    activations, input_grad, total, vec_grad, norm = whole_layer(
        tokens.reshape(seq_length, model_width),
        cotangent.reshape(seq_length, model_width),
        segment_ids,
        attention_weight,
        inner_weight,
        outer_weight,
        vectors,
        ORDER,
        ALPHA_GATHER,
        ALPHA_SCATTER,
    )
    found = adam_step(
        activations,
        input_grad,
        norm,
        vec_grad,
        total,
        (attention_weight, attention_first, attention_second),
        (inner_weight, inner_first, inner_second),
        (outer_weight, outer_first, outer_second),
        (vectors, vector_first, vector_second),
    )
    return (found[0][None], found[1][None], found[2].reshape(()), *found[3:])


def solution(mesh):
    placed = (
        P(("dp", "fsdp"), None, None),
        P(("dp", "fsdp"), None),
        P(("dp", "fsdp"), None, None),
        P(None, "fsdp", None),
        P(None, "fsdp", None),
        P(None, "fsdp", None),
        P("fsdp", None),
        P("fsdp", None),
        P("fsdp", None),
        P("fsdp", None),
        P("fsdp", None),
        P("fsdp", None),
        P(None, "fsdp"),
        P(None, "fsdp"),
        P(None, "fsdp"),
    )
    fused = mesh.shape["dp"] == 4 and mesh.shape["fsdp"] == 8
    return jax.shard_map(
        fused_body if fused else plain_body,
        mesh=mesh,
        in_specs=placed,
        out_specs=(
            P(("dp", "fsdp"), None, None),
            P(("dp", "fsdp"), None, None),
            P(),
            P(None, "fsdp", None),
            P(None, "fsdp", None),
            P(None, "fsdp", None),
            P("fsdp", None),
            P("fsdp", None),
            P("fsdp", None),
            P("fsdp", None),
            P("fsdp", None),
            P("fsdp", None),
            P(None, "fsdp"),
            P(None, "fsdp"),
            P(None, "fsdp"),
            P(None, "fsdp"),
        ),
        check_vma=False,
    )
```

profile of v0, /device:TPU:0, one launch (start us, length us, event | category | flops | bytes accessed | tf_op | source)
XLA Modules:
  0.0 158.7 jit_solution(3470843995076577248)
XLA Ops:
  0.6 146.1 %layer.1 = (bf16[512,768]{1,0:T(8,128)(2,1)}, f32[512,768]{1,0:T(8,128)}, bf16[12,96,768]{2,1,0:T(8,128)(2,1)}, f32[16,768]{1,0:T(8,128)}, f32[8,128]{1,0:T(8,128)}) custom-call(bf16[512,768]{1,0:T(8,128)(2,1)} %bitcast.5, bf16[512,768]{1,0:T(8,128)(2,1)} %bitcast.6, s32[1,512]{1,0:T(1,128)} %seg_h.1, f32[4,96,768]{2,1,0:T(8,128)} %att_w.1, ...), custom_call_target="tpu_custom_call" | custom-call | tf_op jit(solution)/shard_map/layer/pallas_call | solution.py:866
  146.7 11.5 %adam.1 = (bf16[512,768]{1,0:T(8,128)(2,1)}, f32[512,768]{1,0:T(8,128)}, f32[1,1]{1,0:T(1,128)}, f32[4,96,768]{2,1,0:T(8,128)}, f32[4,96,768]{2,1,0:T(8,128)}, /...) custom-call(bf16[512,768]{1,0:T(8,128)(2,1)} %get-tuple-element.37.a, ...), custom_call_target="tpu_custom_call" | custom-call | tf_op jit(solution)/shard_map/adam/pallas_call | solution.py:974
where the time goes:
time: 162 us; the launch traced here: 159 us
  Pallas kernels  158 us (98%)
    pallas_call x1, Pallas kernels, whole_layer(): pl.pallas_call(functools.partial(layer_kernel, order, alpha_gather, alpha...  146 us
    pallas_call x1, Pallas kernels, adam_step(): pl.pallas_call(adam_kernel, out_shape=[jax.ShapeDtypeStruct(activations.s...  11.5 us

commit v1 on v0

--- a/solution.py
+++ b/solution.py
@@ -914,13 +914,17 @@
     def store(p, m):
         return pltpu.make_async_copy(slot(p, m), parts[p][1][m][1], stores.at[p, m])
 
-    load_grads = pltpu.make_async_copy(total_h, grads, loads.at[6, 0])
+    load_grads = [
+        pltpu.make_async_copy(total_h.at[pl.ds(first, 4)], grads.at[pl.ds(first, 4)], loads.at[7, k])
+        for k, first in enumerate((8, 0, 4))
+    ]
     moves = [
         (pltpu.make_async_copy(src, mid, loads.at[6, k]), pltpu.make_async_copy(mid, dst, stores.at[6, k]))
         for k, (src, mid, dst) in enumerate(((act_h, act, act_new), (back_h, back, back_new)), 1)
     ]
-    load_grads.start()
     for p in range(6):
+        if p % 2 == 0:
+            load_grads[p // 2].start()
         for m in range(3):
             load(p, m).start()
         if p == 1:
@@ -938,8 +942,9 @@
     for ref, value in zip((vec_wn, vec_mn, vec_vn), found):
         ref[...] = value
     vec_gn[...] = grad * factor
-    load_grads.wait()
     for p in range(6):
+        if p % 2 == 0:
+            load_grads[p // 2].wait()
         for m in range(3):
             load(p, m).wait()
         for k in range(2):
@@ -981,7 +986,7 @@
         out_specs=[far, far, near, *[far] * 9, *[near] * 4],
         scratch_shapes=[
             hold, vmem(total.shape, BF16), vmem(activations.shape, BF16), vmem(input_grad.shape, F32),
-            dma((7, 3)), dma((7, 3)),
+            dma((8, 3)), dma((7, 3)),
         ],
         compiler_params=pltpu.CompilerParams(vmem_limit_bytes=63 * 2**20),
         name="adam",
@@ -999,20 +1004,20 @@
     ("a1", 4), ("at", 0), ("t1", 2), ("at", 1), ("t2", 3), ("a2", 2), ("a0", 5), ("t2", 2), ("at", 2),
     ("t3", 3), ("a2", 4), ("at", 3), ("t3", 2), ("t0", 4), ("f", 2), ("a1", 5), ("at", 4), ("t1", 4),
     ("f", 3), ("t0", 5), ("at", 5), ("t2", 4), ("wo", 0), ("t3", 4), ("g", 2), ("g", 3), ("a2", 5), ("F", 2),
-    ("F", 3), ("f", 4), ("t1", 5), ("F", 0), ("t2", 5), ("t3", 5), ("f", 5), ("g", 4), ("F", 1), ("g", 5),
-    ("o", 4), ("o", 5), ("ln2", 0), ("agf", 0), ("D", 1), ("G", 0), ("s1", 0), ("G", 1), ("p2", 0), ("s1", 1),
-    ("r1", 1), ("D", 0), ("D", 2), ("D", 3), ("p3", 0), ("p1", 0), ("r1", 0), ("H", 0), ("q2", 0), ("H", 1),
-    ("H", 2), ("G", 2), ("G", 3), ("s1", 2), ("r1", 2), ("p1", 2), ("H", 3), ("ln1", 0), ("p2", 2), ("q3", 0),
-    ("dc", 0), ("p2", 1), ("p3", 2), ("s1", 3), ("ab", 0), ("p0", 0), ("ab", 1), ("r1", 3), ("ab", 2),
-    ("ab", 3), ("q2", 2), ("ab", 4), ("ab", 5), ("dq", 0), ("q1", 0), ("p1", 3), ("p3", 1), ("q0", 0),
-    ("G", 4), ("s1", 4), ("p1", 1), ("p3", 3), ("q2", 1), ("p0", 2), ("q3", 2), ("V", 0), ("q1", 2),
-    ("p0", 3), ("G", 5), ("q1", 3), ("p2", 3), ("p1", 4), ("s1", 5), ("ig", 0), ("V", 1), ("p0", 1),
-    ("q3", 3), ("r1", 4), ("q3", 1), ("q1", 1), ("q0", 3), ("r1", 5), ("p3", 4), ("q2", 3), ("p2", 4),
-    ("q0", 1), ("p2", 5), ("p1", 5), ("V", 2), ("s4", 0), ("q1", 4), ("p0", 4), ("q2", 4), ("q0", 4),
-    ("q2", 5), ("q0", 2), ("p3", 5), ("s4", 2), ("s4", 3), ("q1", 5), ("p0", 5), ("q3", 5), ("q3", 4),
-    ("q0", 5), ("s4", 1), ("V", 3), ("s4", 5), ("s5", 0), ("s5", 2), ("s4", 4), ("s5", 3), ("N", 0), ("V", 4),
-    ("s5", 1), ("s5", 5), ("N", 1), ("s6", 3), ("s6", 0), ("s6", 1), ("s5", 4), ("s6", 4), ("s6", 2),
-    ("N", 2), ("s6", 5), ("fin", 0),
+    ("F", 3), ("f", 4), ("t1", 5), ("F", 0), ("t2", 5), ("t3", 5), ("f", 5), ("g", 4), ("F", 1), ("o", 4),
+    ("g", 5), ("o", 5), ("ln2", 0), ("D", 1), ("G", 0), ("s1", 0), ("G", 1), ("p2", 0), ("s1", 1), ("r1", 1),
+    ("D", 0), ("D", 2), ("D", 3), ("p3", 0), ("p1", 0), ("r1", 0), ("H", 0), ("q2", 0), ("H", 1), ("H", 2),
+    ("agf", 0), ("G", 2), ("G", 3), ("s1", 2), ("r1", 2), ("p1", 2), ("H", 3), ("ln1", 0), ("p2", 2),
+    ("q3", 0), ("dc", 0), ("p2", 1), ("p3", 2), ("s1", 3), ("ab", 0), ("p0", 0), ("ab", 1), ("r1", 3),
+    ("ab", 2), ("ab", 3), ("q2", 2), ("ab", 4), ("ab", 5), ("dq", 0), ("q1", 0), ("p1", 3), ("p3", 1),
+    ("q0", 0), ("G", 4), ("s1", 4), ("p1", 1), ("p3", 3), ("q2", 1), ("p0", 2), ("q3", 2), ("V", 0),
+    ("q1", 2), ("p0", 3), ("G", 5), ("q1", 3), ("p2", 3), ("p1", 4), ("s1", 5), ("ig", 0), ("V", 1),
+    ("p0", 1), ("q3", 3), ("r1", 4), ("q3", 1), ("q1", 1), ("q0", 3), ("r1", 5), ("p3", 4), ("q2", 3),
+    ("p2", 4), ("q0", 1), ("p2", 5), ("p1", 5), ("V", 2), ("s4", 0), ("q1", 4), ("p0", 4), ("q2", 4),
+    ("q0", 4), ("q2", 5), ("q0", 2), ("p3", 5), ("s4", 2), ("s4", 3), ("q1", 5), ("p0", 5), ("q3", 5),
+    ("q3", 4), ("q0", 5), ("s4", 1), ("V", 3), ("s4", 5), ("s5", 0), ("s5", 2), ("s4", 4), ("s5", 3),
+    ("N", 0), ("V", 4), ("s5", 1), ("s5", 5), ("N", 1), ("s6", 3), ("s6", 0), ("s6", 1), ("s5", 4), ("s6", 4),
+    ("s6", 2), ("N", 2), ("s6", 5), ("fin", 0),
 )
 
 def plain_body(

time: 162 us -> 160 us (0.988)
  Pallas kernels: 158 us -> 156 us
where the time goes in v1:
time: 160 us; the launch traced here: 158 us
  Pallas kernels  156 us (98%)
    pallas_call x1, Pallas kernels, whole_layer(): pl.pallas_call(functools.partial(layer_kernel, order, alpha_gather, alpha...  146 us
    pallas_call x1, Pallas kernels, adam_step(): pl.pallas_call(adam_kernel, out_shape=[jax.ShapeDtypeStruct(activations.s...  10.8 us

profile of v1, /device:TPU:0, one launch (start us, length us, event | category | flops | bytes accessed | tf_op | source)
XLA Modules:
  0.0 157.5 jit_solution(62226960905705090)
XLA Ops:
  0.6 145.6 %layer.1 = (bf16[512,768]{1,0:T(8,128)(2,1)}, f32[512,768]{1,0:T(8,128)}, bf16[12,96,768]{2,1,0:T(8,128)(2,1)}, f32[16,768]{1,0:T(8,128)}, f32[8,128]{1,0:T(8,128)}) custom-call(bf16[512,768]{1,0:T(8,128)(2,1)} %bitcast.5, bf16[512,768]{1,0:T(8,128)(2,1)} %bitcast.6, s32[1,512]{1,0:T(1,128)} %seg_h.1, f32[4,96,768]{2,1,0:T(8,128)} %att_w.1, ...), custom_call_target="tpu_custom_call" | custom-call | tf_op jit(solution)/shard_map/layer/pallas_call | solution.py:866
  146.3 10.8 %adam.1 = (bf16[512,768]{1,0:T(8,128)(2,1)}, f32[512,768]{1,0:T(8,128)}, f32[1,1]{1,0:T(1,128)}, f32[4,96,768]{2,1,0:T(8,128)}, f32[4,96,768]{2,1,0:T(8,128)}, /...) custom-call(bf16[512,768]{1,0:T(8,128)(2,1)} %get-tuple-element.37.a, ...), custom_call_target="tpu_custom_call" | custom-call | tf_op jit(solution)/shard_map/adam/pallas_call | solution.py:979
